TPU v7x, 128 devices: a whole 4x4x4 slice. The times are simulated.
128 devices in a mesh: dp: 8 (over y, core), tile: 16 (over z, x).
Axes of the slice: x: 4, y: 4, z: 4, core: 2. Of those that a mesh axis runs over, the one named last changes fastest.
Arguments:
- gate_pre: bfloat16 [3072, 14336], P('dp', 'tile'), may hold values from -6 to 6
- up_pre: bfloat16 [3072, 14336], P('dp', 'tile'), may hold values from -6 to 6
- grad_hidden: bfloat16 [3072, 14336], P('dp', 'tile'), may hold values from -6 to 6
- doc_tokens: int32 [32], replicated, may hold values from 1 to 381, as said below
- doc_shard: int32 [32], replicated, may hold values from 0 to 7, as said below
Outputs:
- act_factor: float32 [14336, 8, 1792], P('tile', 'dp')
- grad_factor: float32 [14336, 8, 1792], P('tile', 'dp')
Inputs may be any that keep to these rules, and one draw needn't show every extreme that they name: `doc_tokens`: each data shard holds exactly 4 documents whose tokens together fill its first slots; the documents of one shard total at most 384 tokens, exactly 384 on one shard, and all documents together hold 2048 tokens. One document holds exactly 381 tokens. `doc_shard`: each data shard index appears exactly 4 times.
All inputs are finite; a program needn't handle non-finite values.
Results may differ from a plain program's by a relative error of at most 0.0039.
Values may be sent and summed in bfloat16 or wider, within the bound.
A program may use at most 128 MiB of HBM per device.

v0:
```python
import jax
import jax.numpy as jnp
from jax import lax
from jax.sharding import PartitionSpec as P

TOK_DEV = 256


def on_device(gate_pre, up_pre, grad_hidden, doc_tokens, doc_shard):
    shards = lax.axis_size("dp")
    capacity = gate_pre.shape[0]
    own_index = lax.axis_index("dp")
    owners = jnp.arange(shards, dtype=jnp.int32)
    shard_loads = jnp.sum(
        jnp.where(doc_shard[None, :] == owners[:, None], doc_tokens[None, :], 0), axis=1
    )
    own_load = jnp.sum(jnp.where(owners == own_index, shard_loads, 0))
    live_rows = (jnp.arange(capacity, dtype=jnp.int32) < own_load)[:, None]
    gate_float = gate_pre.astype(jnp.float32)
    up_float = up_pre.astype(jnp.float32)
    grad_float = grad_hidden.astype(jnp.float32)
    sigmoid_gate = jax.nn.sigmoid(gate_float)
    hidden = jnp.where(live_rows, gate_float * sigmoid_gate * up_float, 0.0).astype(jnp.bfloat16)
    dgate = jnp.where(
        live_rows,
        grad_float * up_float * sigmoid_gate * (1.0 + gate_float * (1.0 - sigmoid_gate)),
        0.0,
    ).astype(jnp.bfloat16)
    stacked = jnp.stack([hidden, dgate])
    pieces = lax.all_to_all(stacked, "dp", split_axis=2, concat_axis=1, tiled=True)
    panel = lax.all_gather(pieces, "dp", axis=2, tiled=True)
    grams = jnp.einsum(
        "frc,frw->fcw",
        panel,
        lax.all_gather(pieces, "tile", axis=2, tiled=True),
        preferred_element_type=jnp.float32,
    )
    scaled = grams * (1.0 / (TOK_DEV * shards))
    rows_here = scaled.shape[1]
    act_factor = scaled[0].reshape(rows_here, 1, scaled.shape[2])
    grad_factor = scaled[1].reshape(rows_here, 1, scaled.shape[2])
    return (act_factor, grad_factor)


def solution(mesh):
    return jax.shard_map(
        on_device,
        mesh=mesh,
        in_specs=(P("dp", "tile"), P("dp", "tile"), P("dp", "tile"), P(), P()),
        out_specs=(P("tile", "dp", None), P("tile", "dp", None)),
        check_vma=False,
    )
```

profile of v0, /device:TPU:0, one launch (start us, length us, event | category | flops | bytes accessed | tf_op | source)
XLA Modules:
  0.0 309.3 jit_solution(12944240311071915761)
XLA Ops:
  7.2 0.0 all-gather.3.cloned.1.call-start
  7.2 0.8 select_reduce_fusion
  8.0 0.6 fusion.12
  8.6 0.6 iota_compare_fusion.1
  9.3 2.4 fusion.10
  11.7 0.1 pad_maximum_fusion
  11.9 2.6 copy.29
  14.5 24.0 %all_to_all.18 = bf16[2,384,896]{1,0,2:T(2,128)(2,1)S(1)} all-to-all(bf16[2,384,896]{1,0,2:T(2,128)(2,1)S(1)} %copy.29), channel_id=1, replica_groups=mesh['dp'=8,'tile'=16] {'dp'}, dimensions={2} | all-to-all | bytes 2752512 | tf_op jit(solution)/shard_map/all_to_all | solution.py:30
  38.5 0.2 copy.30
  38.7 1.3 copy.34
  40.0 0.0 all-gather.3.cloned.1.call-update
  40.0 0.0 all-gather.5.cloned.1.call-start
  40.1 0.7 all-gather.5.cloned.1.call-update
  40.8 60.5 %all-gather.3.cloned.1.call-done = bf16[2,3072,896]{1,2,0:T(8,128)(2,1)} async-done(((bf16[2,3072,112]{1,2,0:T(8,128)(2,1)}), bf16[2,3072,896]{1,2,0:T(8,128)(2,1)}) %all-gather.3.cloned.1.call-update) | async-done | bytes 11010064 | tf_op jit(solution)/shard_map/all_gather | solution.py:31
  101.3 141.3 %all-gather.5.cloned.1.call-done = bf16[2,3072,1792]{1,2,0:T(8,128)(2,1)} async-done(((bf16[2,3072,112]{1,2,0:T(8,128)(2,1)}), bf16[2,3072,1792]{1,2,0:T(8,128)(2,1)}) %all-gather.5.cloned.1.call-update) | async-done | bytes 22020112 | tf_op jit(solution)/shard_map/all_gather | solution.py:35
  242.5 28.3 %broadcast_multiply_fusion = f32[2,896,1792]{2,1,0:T(8,128)} fusion(bf16[2,3072,896]{1,2,0:T(8,128)(2,1)} %all-gather.3.cloned.1.call-done, bf16[2,3072,1792]{1,2,0:T(8,128)(2,1)} %all-gather.5.cloned.1.call-done), kind=kOutput, calls=%fused_computation.2 | convolution fusion | flops 19733217280 | bytes 45875200 | tf_op jit(solution)/shard_map/frc,frw->fcw/dot_general | solution.py:32
  270.8 10.3 %slice_bitcast_fusion = (f32[896,1,1792]{2,0,1:T(8,128)}, f32[896,1,1792]{2,0,1:T(8,128)}) fusion(f32[2,896,1792]{2,1,0:T(8,128)} %broadcast_multiply_fusion), kind=kLoop, calls=%fused_computation | loop fusion | bytes 25690112 | tf_op jit(solution)/shard_map/reshape;squeeze | solution.py:41
  281.1 0.0 copy-start
  281.1 11.1 %copy.33 = f32[896,1,1792]{2,1,0:T(1,128)} copy(f32[896,1,1792]{2,0,1:T(8,128)} %get-tuple-element.12) | data formatting | bytes 12845056
  292.2 0.0 copy-done
  292.2 10.3 %copy.32 = f32[896,1,1792]{2,1,0:T(1,128)} copy(f32[896,1,1792]{2,0,1:T(8,128)S(1)} %copy-done) | data formatting | bytes 12845056
Async XLA Ops:
  7.2 94.1 %all-gather.3.cloned.1.call-start = ((), (), s32[]{:S(2)}) async-start(), calls=%async_computation.1 | async-start | bytes 12386304 | tf_op jit(solution)/shard_map/all_gather | solution.py:31
  40.0 202.5 %all-gather.5.cloned.1.call-start = ((), (), s32[]{:S(2)}) async-start(), calls=%async_computation.2 | async-start | bytes 23396352 | tf_op jit(solution)/shard_map/all_gather | solution.py:35
  281.1 11.1 %copy-start = (f32[896,1,1792]{2,0,1:T(8,128)S(1)}, f32[896,1,1792]{2,0,1:T(8,128)}, u32[]{:S(2)}) copy-start(f32[896,1,1792]{2,0,1:T(8,128)} %get-tuple-element.13) | copy-start | bytes 19267588
Sparse Core Ops, SparseCore 0:
  40.1 61.0 all-gather.2
  104.0 138.5 all-gather.4
where the time goes:
time: 310 us; the launch traced here: 309 us
  waiting for transfers between devices  202 us (65%)
  local copies, waits for them, and re-layouts  35.8 us (12%)
  matrix products  28.3 us (9%)
  blocking collectives  24 us (8%)
  between operations  14.1 us (5%)
  other arithmetic  4.65 us (2%)
    all_gather x1, waiting for transfers between devices, on_device(): lax.all_gather(pieces, 'tile', axis=2, tiled=True)  141 us
    all_gather x1, waiting for transfers between devices, on_device(): panel = lax.all_gather(pieces, 'dp', axis=2, tiled=True)  60.5 us
    dot_general x1, matrix products, on_device(): jnp.einsum('frc,frw->fcw', panel, lax.all_gather(pieces, 'tile', axis=2,...  28.3 us
    all_to_all x1, blocking collectives, on_device(): lax.all_to_all(stacked, 'dp', split_axis=2, concat_axis=1, tiled=True)  24 us
    unnamed x4, local copies, waits for them, and re-layouts  21.4 us
    another operation x1, local copies, waits for them, and re-layouts, on_device(): grad_factor = scaled[1].reshape(rows_here, 1, scaled.shape[2])  10.3 us
  transfers between devices with their start and end apart: 2, of which 2 were waited for; matrix products, arithmetic and copies ran while one was open for 0% of the time, Pallas kernels for 0%

commit v1 on v0

v1 whole, which is shorter than its diff:
```python
import jax
import jax.numpy as jnp
from jax import lax
from jax.experimental import pallas as pl
from jax.experimental.pallas import tpu as pltpu
from jax.sharding import PartitionSpec as P

MESH = pl.DeviceIdType.MESH
TOK_DEV = 256
DOCS_SHARD = 4
WIDE = 256
SIDE = 4


def packing_blocks(shards, capacity, tokens):
    blocks = [[] for _ in range(tokens // WIDE)]
    for shard in range(shards):
        after = shards - shard
        first = max(DOCS_SHARD * shard, tokens - capacity * after)
        last = min(capacity * shard, tokens - DOCS_SHARD * after) + capacity
        for block in range(first // WIDE, -(-min(last, tokens) // WIDE)):
            blocks[block].append(shard)
    return blocks


def make_kernel(capacity, units, group, shards, tiles):
    tokens = TOK_DEV * shards
    blocks = packing_blocks(shards, capacity, tokens)
    slots = {}
    for n, members in enumerate(blocks):
        for shard in members:
            slots[n, shard] = len(slots)
    pieces = 4
    width = tokens // pieces
    columns = tiles * group

    def kernel(tok_ref, own_ref, gate_ref, up_ref, down_ref, act_ref, grad_ref, xt, rv, perm, rp, cp,
               swap_s, swap_r, local_s, row_s, row_r, col_s, col_r):
        outs = (act_ref, grad_ref)
        dp, tile = lax.axis_index("dp"), lax.axis_index("tile")
        y, core = dp // 2, lax.rem(dp, 2)
        z, x = tile // SIDE, lax.rem(tile, SIDE)

        def plus(a, d):
            return lax.rem(a + d + SIDE, SIDE)

        def over_dp(offset):
            return lax.rem(dp + offset + shards, shards)

        def y_peer(d):
            return (plus(y, d) * 2 + core, tile)

        sibling = (y * 2 + 1 - core, tile)

        def plane(first_is_x, d1, d2):
            dx, dz = (d1, d2) if first_is_x else (d2, d1)
            return plus(z, dz) * SIDE + plus(x, dx)

        barrier = pltpu.get_barrier_semaphore()
        peers = [(over_dp(o), tile) for o in range(1, shards)]
        peers += [(dp, plane(True, d, 0)) for d in (1, 2, 3)] + [(dp, plane(True, 0, d)) for d in (1, 2, 3)]
        for peer in peers:
            pl.semaphore_signal(barrier, inc=1, device_id=peer, device_id_type=MESH)

        def count(i, loads):
            return tuple(v + jnp.where(own_ref[i] == j, tok_ref[i], 0) for j, v in enumerate(loads))

        loads = lax.fori_loop(0, shards * DOCS_SHARD, count, (jnp.int32(0),) * shards)
        own_load, offsets, total = jnp.int32(0), [], jnp.int32(0)
        for j in range(shards):
            own_load = own_load + jnp.where(dp == j, loads[j], 0)
            offsets.append(total)
            total = total + loads[j]

        live = lax.broadcasted_iota(jnp.int32, (capacity, 128), 0) < own_load

        def make_hidden(b, _):
            cols = pl.ds(pl.multiple_of(b * 128, 128), 128)
            g = gate_ref[:, cols].astype(jnp.float32)
            u = up_ref[:, cols].astype(jnp.float32)
            h = jnp.where(live, g * jax.nn.sigmoid(g) * u, 0.0)
            xt[0, cols, :] = h.T.astype(jnp.bfloat16)
            return 0

        def make_dgate(b, _):
            cols = pl.ds(pl.multiple_of(b * 128, 128), 128)
            g = gate_ref[:, cols].astype(jnp.float32)
            u = up_ref[:, cols].astype(jnp.float32)
            d = down_ref[:, cols].astype(jnp.float32)
            s = jax.nn.sigmoid(g)
            h = jnp.where(live, d * u * s * (1.0 + g * (1.0 - s)), 0.0)
            xt[1, cols, :] = h.T.astype(jnp.bfloat16)
            return 0

        def at_group(index):
            return pl.ds(pl.multiple_of(index * group, 16), group)

        def swap(f, o):
            return pltpu.make_async_remote_copy(
                src_ref=xt.at[f, at_group(over_dp(o))], dst_ref=rv.at[f, dp],
                send_sem=swap_s.at[f, o], recv_sem=swap_r.at[f, o],
                device_id=(over_dp(o), tile), device_id_type=MESH)

        def swap_in(f, o):
            return pltpu.make_async_remote_copy(
                src_ref=xt.at[f, at_group(dp)], dst_ref=rv.at[f, over_dp(-o)],
                send_sem=swap_s.at[f, o], recv_sem=swap_r.at[f, o],
                device_id=(over_dp(o), tile), device_id_type=MESH)

        def swap_own(f):
            return pltpu.make_async_copy(xt.at[f, at_group(dp)], rv.at[f, dp], local_s.at[f])

        def start_swap(f):
            for o in (3, 4, 5, 2, 6, 7, 1):
                swap(f, o).start()
            swap_own(f).start()

        def end_swap(f):
            swap_own(f).wait()
            for o in range(1, shards):
                swap_in(f, o).wait_recv()

        def build_perm():
            diff = (lax.broadcasted_iota(jnp.int32, (capacity, WIDE), 1)
                    - lax.broadcasted_iota(jnp.int32, (capacity, WIDE), 0))
            for (n, shard), slot in slots.items():
                hit = diff == offsets[shard] - n * WIDE
                perm[slot] = jnp.where(hit, 1.0, 0.0).astype(jnp.bfloat16)

        def pack(f, q):
            for n in range(q * width // WIDE, (q + 1) * width // WIDE):
                acc = None
                for shard in blocks[n]:
                    term = jnp.dot(rv[f, shard], perm[slots[n, shard]], preferred_element_type=jnp.float32)
                    acc = term if acc is None else acc + term
                packed = acc.astype(jnp.bfloat16)
                cp[f, at_group(tile), n * WIDE:(n + 1) * WIDE] = packed
                rp[f, at_group(dp), n * WIDE:(n + 1) * WIDE] = packed

        def row(f, index, origin, peer):
            part = rp.at[f, at_group(origin)]
            return pltpu.make_async_remote_copy(
                src_ref=part, dst_ref=part, send_sem=row_s.at[f, index], recv_sem=row_r.at[f, index],
                device_id=peer, device_id_type=MESH)

        def row_out(f):
            for d in (1, 2, 3):
                row(f, d, dp, y_peer(d)).start()
            row(f, 0, dp, sibling).start()

        def row_pass(f):
            for d in (1, 3, 2):
                origin = plus(y, -d) * 2 + core
                row(f, d, origin, y_peer(d)).wait_recv()
                row(f, SIDE + d, origin, sibling).start()

        def row_end(f):
            for d in range(SIDE):
                index = 0 if d == 0 else SIDE + d
                row(f, index, plus(y, -d) * 2 + 1 - core, sibling).wait_recv()

        def column(f, q, index, origin, peer):
            part = cp.at[f, at_group(origin), pl.ds(q * width, width)]
            return pltpu.make_async_remote_copy(
                src_ref=part, dst_ref=part, send_sem=col_s.at[f, q, index], recv_sem=col_r.at[f, q, index],
                device_id=(dp, peer), device_id_type=MESH)

        def col_out(f, q):
            first = q % 2 == 0
            for d in (1, 3, 2):
                column(f, q, d - 1, tile, plane(first, d, 0)).start()
            for d in (1, 3, 2):
                column(f, q, 2 + d, tile, plane(first, 0, d)).start()

        def col_pass(f, q):
            first = q % 2 == 0
            for b in (1, 3, 2):
                origin = plane(first, -b, 0)
                column(f, q, b - 1, origin, plane(first, b, 0)).wait_recv()
                for d in (1, 3, 2):
                    column(f, q, 2 + b * 3 + d, origin, plane(first, 0, d)).start()

        def col_end(f, q):
            first = q % 2 == 0
            for b in range(SIDE):
                for d in (1, 2, 3):
                    column(f, q, 2 + b * 3 + d, plane(first, -b, -d), plane(first, 0, d)).wait_recv()

        def multiply(f, pair):
            ks = pl.ds(pair * 2 * width, 2 * width)

            def step(n, _):
                cols = pl.ds(pl.multiple_of(n * WIDE, WIDE), WIDE)
                gram = lax.dot_general(rp[f, :, ks], cp[f, cols, ks], (((1,), (1,)), ((), ())),
                                       preferred_element_type=jnp.float32)
                if pair == 0:
                    outs[f][:, cols] = gram
                else:
                    outs[f][:, cols] = (outs[f][:, cols] + gram) * (1.0 / tokens)
                return 0

            lax.fori_loop(0, columns // WIDE, step, 0)

        lax.fori_loop(0, units // 128, make_hidden, 0)
        pl.semaphore_wait(barrier, len(peers))
        start_swap(0)
        lax.fori_loop(0, units // 128, make_dgate, 0)
        build_perm()
        end_swap(0)
        start_swap(1)
        pack(0, 0)
        col_out(0, 0)
        pack(0, 1)
        col_out(0, 1)
        pack(0, 2)
        pack(0, 3)
        col_pass(0, 0)
        col_pass(0, 1)
        col_out(0, 2)
        col_out(0, 3)
        end_swap(1)
        row_out(0)
        for q in range(pieces):
            pack(1, q)
        col_pass(0, 2)
        col_pass(0, 3)
        col_out(1, 0)
        col_out(1, 1)
        row_pass(0)
        row_out(1)
        row_end(0)
        col_end(0, 0)
        col_end(0, 1)
        multiply(0, 0)
        col_pass(1, 0)
        col_pass(1, 1)
        col_out(1, 2)
        col_out(1, 3)
        col_end(0, 2)
        col_end(0, 3)
        multiply(0, 1)
        col_pass(1, 2)
        col_pass(1, 3)
        row_pass(1)
        row_end(1)
        col_end(1, 0)
        col_end(1, 1)
        multiply(1, 0)
        col_end(1, 2)
        col_end(1, 3)
        multiply(1, 1)

        for f in range(2):
            for o in range(1, shards):
                swap(f, o).wait_send()
            for d in range(2 * SIDE):
                if d != SIDE:
                    row(f, d, dp, sibling).wait_send()
            for q in range(pieces):
                for i in range(15):
                    column(f, q, i, tile, plane(True, 1, 0)).wait_send()

    scratch = [
        pltpu.VMEM((2, units, capacity), jnp.bfloat16),
        pltpu.VMEM((2, shards, group, capacity), jnp.bfloat16),
        pltpu.VMEM((len(slots), capacity, WIDE), jnp.bfloat16),
        pltpu.VMEM((2, units, tokens), jnp.bfloat16),
        pltpu.VMEM((2, columns, tokens), jnp.bfloat16),
        pltpu.SemaphoreType.DMA((2, shards)),
        pltpu.SemaphoreType.DMA((2, shards)),
        pltpu.SemaphoreType.DMA((2,)),
        pltpu.SemaphoreType.DMA((2, 2 * SIDE)),
        pltpu.SemaphoreType.DMA((2, 2 * SIDE)),
        pltpu.SemaphoreType.DMA((2, pieces, 15)),
        pltpu.SemaphoreType.DMA((2, pieces, 15)),
    ]
    return kernel, scratch


def solution(mesh):
    shards, tiles = mesh.shape["dp"], mesh.shape["tile"]

    def on_device(gate_pre, up_pre, grad_hidden, doc_tokens, doc_shard):
        capacity, units = gate_pre.shape
        group = units // shards
        kernel, scratch = make_kernel(capacity, units, group, shards, tiles)
        columns = tiles * group
        smem, vmem = pl.BlockSpec(memory_space=pltpu.SMEM), pl.BlockSpec(memory_space=pltpu.VMEM)
        act, grad = pl.pallas_call(
            kernel,
            out_shape=[jax.ShapeDtypeStruct((units, columns), jnp.float32)] * 2,
            in_specs=[smem, smem, vmem, vmem, vmem],
            out_specs=[vmem, vmem],
            scratch_shapes=scratch,
            compiler_params=pltpu.CompilerParams(
                collective_id=0, has_side_effects=True, vmem_limit_bytes=58 << 20),
            name="gram_exchange",
        )(doc_tokens, doc_shard, gate_pre, up_pre, grad_hidden)
        return act.reshape(units, 1, columns), grad.reshape(units, 1, columns)

    return jax.shard_map(
        on_device,
        mesh=mesh,
        in_specs=(P("dp", "tile"), P("dp", "tile"), P("dp", "tile"), P(), P()),
        out_specs=(P("tile", "dp", None), P("tile", "dp", None)),
        check_vma=False,
    )
```

time: 310 us -> 154 us (0.50)
  waiting for transfers between devices: 202 us -> 0 us
  Pallas kernels: 0 us -> 132 us
  matrix products: 28.3 us -> 0 us
  blocking collectives: 24 us -> 0 us
  local copies, waits for them, and re-layouts: 35.8 us -> 21.4 us
  between operations: 14.1 us -> 0.65 us
  other arithmetic: 4.65 us -> 0 us
    all_gather x2 -> x0, waiting for transfers between devices: 202 us -> none  [the longest x1 141 us: on_device(): lax.all_gather(pieces, 'tile', axis=2, tiled=True)]
    pallas_call x0 -> x1, Pallas kernels: none -> 132 us  [on_device(): pl.pallas_call(kernel, out_shape=[jax.ShapeDtypeStruct((units, columns),...]
    dot_general x1 -> x0, matrix products: 28.3 us -> none  [on_device(): jnp.einsum('frc,frw->fcw', panel, lax.all_gather(pieces, 'tile', axis=2,...]
    all_to_all x1 -> x0, blocking collectives: 24 us -> none  [on_device(): lax.all_to_all(stacked, 'dp', split_axis=2, concat_axis=1, tiled=True)]
    another operation x2 -> x0, local copies, waits for them, and re-layouts: 12.9 us -> none  [the longest x1 10.3 us: on_device(): grad_factor = scaled[1].reshape(rows_here, 1, scaled.shape[2])]
  transfers between devices with their start and end apart: 2 -> 0, of which waited for: 2 -> 0; matrix products, arithmetic and copies ran while one was open for 0% -> 0% of each run, Pallas kernels for 0% -> 0%
where the time goes in v1:
time: 154 us
  Pallas kernels  132 us (86%)
  local copies, waits for them, and re-layouts  21.4 us (14%)
    pallas_call x1, Pallas kernels, on_device(): pl.pallas_call(kernel, out_shape=[jax.ShapeDtypeStruct((units, columns),...  132 us
    unnamed x4, local copies, waits for them, and re-layouts  21.4 us

profile of v1, /device:TPU:0, one launch (start us, length us, event | category | flops | bytes accessed | tf_op | source)
XLA Modules:
  0.0 153.6 jit_solution(10177107949530448222)
XLA Ops:
  0.6 131.5 %gram_exchange.1 = (f32[896,1792]{1,0:T(8,128)}, f32[896,1792]{1,0:T(8,128)}) custom-call(s32[32]{0:T(128)} %tok_ref.1, s32[32]{0:T(128)} %own_ref.1, bf16[384,896]{1,0:T(8,128)(2,1)} %gate_ref.1, bf16[384,896]{1,0:T(8,128)(2,1)} %up_ref.1, bf16[384,896]{1,0:T(8,128)(2,1)} %down_ref.1), custom_call_target="tpu_custom_call" | custom-call | tf_op jit(solution)/shard_map/gram_exchange/pallas_call | solution.py:289
  132.2 0.0 copy-start
  132.2 11.1 %copy.7 = f32[896,1,1792]{2,1,0:T(1,128)} copy(f32[896,1,1792]{2,0,1:T(8,128)} %bitcast.3) | data formatting | bytes 12845056
  143.3 0.0 copy-done
  143.3 10.3 %copy.8 = f32[896,1,1792]{2,1,0:T(1,128)} copy(f32[896,1,1792]{2,0,1:T(8,128)S(1)} %bitcast.2) | data formatting | bytes 12845056
Async XLA Ops:
  132.2 11.1 %copy-start = (f32[896,1792]{1,0:T(8,128)S(1)}, f32[896,1792]{1,0:T(8,128)}, u32[]{:S(2)}) copy-start(f32[896,1792]{1,0:T(8,128)} %get-tuple-element.5) | copy-start | bytes 19267588

commit v2 on v1

v2 whole, which is shorter than its diff:
```python
import jax
import jax.numpy as jnp
from jax import lax
from jax.experimental import pallas as pl
from jax.experimental.pallas import tpu as pltpu
from jax.sharding import PartitionSpec as P

MESH = pl.DeviceIdType.MESH
TOK_DEV = 256
DOCS_SHARD = 4
F1_WIDTHS = (512, 256, 256)
WIDE = 256
SIDE = 4


def packing_blocks(shards, capacity, tokens):
    blocks = [[] for _ in range(tokens // WIDE)]
    for shard in range(shards):
        after = shards - shard
        first = max(DOCS_SHARD * shard, tokens - capacity * after)
        last = min(capacity * shard, tokens - DOCS_SHARD * after) + capacity
        for block in range(first // WIDE, -(-min(last, tokens) // WIDE)):
            blocks[block].append(shard)
    return blocks


def make_kernel(capacity, units, group, shards, tiles):
    tokens = TOK_DEV * shards
    blocks = packing_blocks(shards, capacity, tokens)
    slots = {}
    for n, members in enumerate(blocks):
        for shard in members:
            slots[n, shard] = len(slots)
    half = tokens // 2
    cut = group * 3 // 7
    parts = [(0, 0, cut), (0, cut, group - cut), (1, 0, group)]
    pieces = []
    for f, top, rows in parts[:2]:
        pieces += [(f, top, rows, 0, half), (f, top, rows, half, half)]
    start = 0
    for wide in F1_WIDTHS:
        pieces += [(1, 0, group, start, wide), (1, 0, group, start + wide, wide)]
        start += 2 * wide
    pairs = [(i, i + 1) for i in range(0, len(pieces), 2)]
    columns = tiles * group

    def kernel(tok_ref, own_ref, gate_ref, up_ref, down_ref, act_ref, grad_ref, rp1, cp1, xt, rv, perm, rp0, cp0,
               swap_s, swap_r, local_s, row_s, row_r, col_s, col_r):
        outs, rp, cp = (act_ref, grad_ref), (rp0, rp1), (cp0, cp1)
        sent = []

        def send(copy):
            copy.start()
            sent.append(copy)

        dp, tile = lax.axis_index("dp"), lax.axis_index("tile")
        y, core = dp // 2, lax.rem(dp, 2)
        z, x = tile // SIDE, lax.rem(tile, SIDE)

        def plus(a, d):
            return lax.rem(a + d + SIDE, SIDE)

        def over_dp(offset):
            return lax.rem(dp + offset + shards, shards)

        def y_peer(d):
            return (plus(y, d) * 2 + core, tile)

        sibling = (y * 2 + 1 - core, tile)

        def plane(first_is_x, d1, d2):
            dx, dz = (d1, d2) if first_is_x else (d2, d1)
            return plus(z, dz) * SIDE + plus(x, dx)

        barrier = pltpu.get_barrier_semaphore()
        peers = [(over_dp(o), tile) for o in range(1, shards)]
        peers += [(dp, plane(True, d, 0)) for d in (1, 2, 3)] + [(dp, plane(True, 0, d)) for d in (1, 2, 3)]
        for peer in peers:
            pl.semaphore_signal(barrier, inc=1, device_id=peer, device_id_type=MESH)

        def count(i, loads):
            return tuple(v + jnp.where(own_ref[i] == j, tok_ref[i], 0) for j, v in enumerate(loads))

        loads = lax.fori_loop(0, shards * DOCS_SHARD, count, (jnp.int32(0),) * shards)
        own_load, offsets, total = jnp.int32(0), [], jnp.int32(0)
        for j in range(shards):
            own_load = own_load + jnp.where(dp == j, loads[j], 0)
            offsets.append(total)
            total = total + loads[j]

        live = lax.broadcasted_iota(jnp.int32, (capacity, 128), 0) < own_load

        def make_hidden(b, _):
            cols = pl.ds(pl.multiple_of(b * 128, 128), 128)
            g = gate_ref[:, cols].astype(jnp.float32)
            u = up_ref[:, cols].astype(jnp.float32)
            h = jnp.where(live, g * jax.nn.sigmoid(g) * u, 0.0)
            xt[0, cols, :] = h.T.astype(jnp.bfloat16)
            return 0

        def make_dgate(b, _):
            cols = pl.ds(pl.multiple_of(b * 128, 128), 128)
            g = gate_ref[:, cols].astype(jnp.float32)
            u = up_ref[:, cols].astype(jnp.float32)
            d = down_ref[:, cols].astype(jnp.float32)
            s = jax.nn.sigmoid(g)
            h = jnp.where(live, d * u * s * (1.0 + g * (1.0 - s)), 0.0)
            xt[1, cols, :] = h.T.astype(jnp.bfloat16)
            return 0

        def at_group(index):
            return pl.ds(pl.multiple_of(index * group, 16), group)

        def rows_of(index, top, rows):
            return pl.ds(pl.multiple_of(index * group + top, 16), rows)

        def swap(part, o, source, home):
            f, top, rows = parts[part]
            return pltpu.make_async_remote_copy(
                src_ref=xt.at[f, rows_of(home, top, rows)], dst_ref=rv.at[f, source, pl.ds(top, rows)],
                send_sem=swap_s.at[part, o], recv_sem=swap_r.at[part, o],
                device_id=(over_dp(o), tile), device_id_type=MESH)

        def swap_own(part):
            f, top, rows = parts[part]
            return pltpu.make_async_copy(
                xt.at[f, rows_of(dp, top, rows)], rv.at[f, dp, pl.ds(top, rows)], local_s.at[part])

        def start_swap(part):
            for o in (3, 4, 5, 2, 6, 7, 1):
                send(swap(part, o, dp, over_dp(o)))
            swap_own(part).start()

        def end_swap(part):
            swap_own(part).wait()
            for o in range(1, shards):
                swap(part, o, over_dp(-o), dp).wait_recv()

        def build_perm():
            diff = (lax.broadcasted_iota(jnp.int32, (capacity, WIDE), 1)
                    - lax.broadcasted_iota(jnp.int32, (capacity, WIDE), 0))
            for (n, shard), slot in slots.items():
                hit = diff == offsets[shard] - n * WIDE
                perm[slot] = jnp.where(hit, 1.0, 0.0).astype(jnp.bfloat16)

        def pack(piece):
            f, top, rows, start, wide = pieces[piece]
            for n in range(start // WIDE, (start + wide) // WIDE):
                acc = None
                for shard in blocks[n]:
                    term = jnp.dot(rv[f, shard, top:top + rows], perm[slots[n, shard]],
                                   preferred_element_type=jnp.float32)
                    acc = term if acc is None else acc + term
                packed = acc.astype(jnp.bfloat16)
                cp[f][rows_of(tile, top, rows), n * WIDE:(n + 1) * WIDE] = packed
                rp[f][rows_of(dp, top, rows), n * WIDE:(n + 1) * WIDE] = packed

        def row(f, index, origin, peer):
            lanes = pl.ds((index - 2) * half, half) if index in (2, 3) else slice(None)
            part = rp[f].at[at_group(origin), lanes]
            return pltpu.make_async_remote_copy(
                src_ref=part, dst_ref=part, send_sem=row_s.at[f, index], recv_sem=row_r.at[f, index],
                device_id=peer, device_id_type=MESH)

        def same_core(d):
            return plus(y, d) * 2 + core

        def row_out(f):
            send(row(f, 0, dp, y_peer(1)))
            send(row(f, 1, dp, y_peer(-1)))
            send(row(f, 4, dp, sibling))

        def row_pass(f):
            for index, d in ((0, 1), (1, -1)):
                row(f, index, same_core(-d), sibling).wait_recv()
                send(row(f, 2 + index, same_core(-d), y_peer(d)))
                send(row(f, 5 + index, same_core(-d), sibling))

        def row_far(f):
            for index in (2, 3):
                row(f, index, same_core(2), sibling).wait_recv()
            send(row(f, 7, same_core(2), sibling))

        def row_end(f):
            for index, d in ((4, 0), (5, -1), (6, 1), (7, 2)):
                row(f, index, plus(y, d) * 2 + 1 - core, sibling).wait_recv()

        def column(piece, index, origin, peer):
            f, top, rows, start, wide = pieces[piece]
            kind = index % 4
            if kind >= 2:
                wide = wide // 2
                start += (kind - 2) * wide
            part = cp[f].at[rows_of(origin, top, rows), pl.ds(start, wide)]
            return pltpu.make_async_remote_copy(
                src_ref=part, dst_ref=part, send_sem=col_s.at[piece, index], recv_sem=col_r.at[piece, index],
                device_id=(dp, peer), device_id_type=MESH)

        def place(piece, d1, d2):
            return plane(piece % 2 == 0, d1, d2)

        def col_out(p):
            for index, d in ((0, 1), (1, -1)):
                send(column(p, index, tile, place(p, d, 0)))
            for index, d in ((4, 1), (5, -1)):
                send(column(p, index, tile, place(p, 0, d)))

        def col_near(p):
            for index, d in ((0, 1), (1, -1)):
                origin = place(p, -d, 0)
                column(p, index, origin, tile).wait_recv()
                send(column(p, 2 + index, origin, place(p, d, 0)))
            for b, d in ((1, 1), (3, -1)):
                origin = place(p, -d, 0)
                send(column(p, 4 + 4 * b, origin, place(p, 0, 1)))
                send(column(p, 5 + 4 * b, origin, place(p, 0, -1)))

        def col_far(p):
            origin = place(p, 2, 0)
            for index in (2, 3):
                column(p, index, origin, tile).wait_recv()
            send(column(p, 12, origin, place(p, 0, 1)))
            send(column(p, 13, origin, place(p, 0, -1)))

        def col_pass(p, b):
            for index, d in ((0, 1), (1, -1)):
                origin = place(p, -b, -d)
                column(p, 4 + 4 * b + index, origin, tile).wait_recv()
                send(column(p, 6 + 4 * b + index, origin, place(p, 0, d)))

        def col_end(p):
            for b in range(SIDE):
                for index in (2, 3):
                    column(p, 4 + 4 * b + index, place(p, -b, 2), tile).wait_recv()

        def multiply(f, start, wide, first, last):
            ks = pl.ds(start, wide)

            def step(n, _):
                cols = pl.ds(pl.multiple_of(n * WIDE, WIDE), WIDE)
                gram = lax.dot_general(rp[f][:, ks], cp[f][cols, ks], (((1,), (1,)), ((), ())),
                                       preferred_element_type=jnp.float32)
                if start > 0:
                    gram = outs[f][:, cols] + gram
                if start + wide == tokens:
                    gram = gram * (1.0 / tokens)
                outs[f][:, cols] = gram
                return 0

            lax.fori_loop(first, last, step, 0)

        def each(act, pair, *more):
            for p in pairs[pair]:
                act(p, *more)

        lax.fori_loop(0, units // 128, make_hidden, 0)
        pl.semaphore_wait(barrier, len(peers))
        start_swap(0)
        build_perm()
        end_swap(0)
        start_swap(1)
        for p in pairs[0]:
            pack(p)
            col_out(p)
        lax.fori_loop(0, units // 128, make_dgate, 0)
        end_swap(1)
        start_swap(2)
        each(pack, 1)
        each(col_near, 0)
        each(col_out, 1)
        each(col_pass, 0, 0)
        each(col_far, 0)
        end_swap(2)
        row_out(0)
        each(col_pass, 0, 1)
        each(col_pass, 0, 3)
        each(pack, 2)
        each(pack, 3)
        each(pack, 4)
        each(col_pass, 0, 2)
        each(col_near, 1)
        each(col_out, 2)
        row_pass(0)
        each(col_pass, 1, 0)
        each(col_far, 1)
        each(col_pass, 1, 1)
        row_far(0)
        row_out(1)
        each(col_pass, 1, 3)
        each(col_pass, 1, 2)
        row_end(0)
        each(col_near, 2)
        each(col_out, 3)
        each(col_end, 0)
        each(col_end, 1)
        multiply(0, 0, tokens, 0, 2)
        row_pass(1)
        each(col_pass, 2, 0)
        each(col_far, 2)
        multiply(0, 0, tokens, 2, 4)
        each(col_pass, 2, 1)
        each(col_pass, 2, 3)
        multiply(0, 0, tokens, 4, 5)
        row_far(1)
        each(col_pass, 2, 2)
        each(col_near, 3)
        each(col_out, 4)
        multiply(0, 0, tokens, 5, 7)
        row_end(1)
        each(col_pass, 3, 0)
        each(col_far, 3)
        each(col_end, 2)
        each(col_pass, 3, 1)
        each(col_pass, 3, 3)
        multiply(1, 0, 2 * F1_WIDTHS[0], 0, 4)
        each(col_pass, 3, 2)
        each(col_near, 4)
        multiply(1, 0, 2 * F1_WIDTHS[0], 4, 7)
        each(col_pass, 4, 0)
        each(col_far, 4)
        each(col_pass, 4, 1)
        each(col_pass, 4, 3)
        each(col_pass, 4, 2)
        each(col_end, 3)
        multiply(1, 2 * F1_WIDTHS[0], 2 * F1_WIDTHS[1], 0, 7)
        each(col_end, 4)
        for copy in sent:
            copy.wait_send()

    vmem = pltpu.VMEM
    outputs = [
        vmem((units, columns), jnp.float32),
        vmem((units, columns), jnp.float32),
        vmem((units, tokens), jnp.bfloat16),
        vmem((columns, tokens), jnp.bfloat16),
    ]
    scratch = [
        vmem((2, units, capacity), jnp.bfloat16),
        vmem((2, shards, group, capacity), jnp.bfloat16),
        vmem((len(slots), capacity, WIDE), jnp.bfloat16),
        vmem((units, tokens), jnp.bfloat16),
        vmem((columns, tokens), jnp.bfloat16),
        pltpu.SemaphoreType.DMA((len(parts), shards)),
        pltpu.SemaphoreType.DMA((len(parts), shards)),
        pltpu.SemaphoreType.DMA((len(parts),)),
        pltpu.SemaphoreType.DMA((2, 8)),
        pltpu.SemaphoreType.DMA((2, 8)),
        pltpu.SemaphoreType.DMA((len(pieces), 20)),
        pltpu.SemaphoreType.DMA((len(pieces), 20)),
    ]
    return kernel, outputs, scratch


def make_finish(units, columns, tokens):
    last = 2 * F1_WIDTHS[-1]

    def finish(act_in, grad_in, rp, cp, act_ref, grad_ref, total, act_s, grad_s):
        act_out = pltpu.make_async_copy(act_in, act_ref.at[:, 0, :], act_s)
        act_out.start()

        def copy(n):
            cols = pl.ds(pl.multiple_of(n * WIDE, WIDE), WIDE)
            return pltpu.make_async_copy(total.at[:, cols], grad_ref.at[:, 0, cols], grad_s.at[n])

        def step(n, _):
            cols = pl.ds(pl.multiple_of(n * WIDE, WIDE), WIDE)
            ks = pl.ds(tokens - last, last)
            gram = lax.dot_general(rp[:, ks], cp[cols, ks], (((1,), (1,)), ((), ())),
                                   preferred_element_type=jnp.float32)
            total[:, cols] = (grad_in[:, cols] + gram) * (1.0 / tokens)
            copy(n).start()
            return 0

        def wait(n, _):
            copy(n).wait()
            return 0

        lax.fori_loop(0, columns // WIDE, step, 0)
        lax.fori_loop(0, columns // WIDE, wait, 0)
        act_out.wait()

    scratch = [
        pltpu.VMEM((units, columns), jnp.float32),
        pltpu.SemaphoreType.DMA,
        pltpu.SemaphoreType.DMA((columns // WIDE,)),
    ]
    return finish, scratch


def solution(mesh):
    shards, tiles = mesh.shape["dp"], mesh.shape["tile"]

    def on_device(gate_pre, up_pre, grad_hidden, doc_tokens, doc_shard):
        capacity, units = gate_pre.shape
        group = units // shards
        columns = tiles * group
        kernel, outputs, scratch = make_kernel(capacity, units, group, shards, tiles)
        smem, vmem = pl.BlockSpec(memory_space=pltpu.SMEM), pl.BlockSpec(memory_space=pltpu.VMEM)
        panels = pl.pallas_call(
            kernel,
            out_shape=outputs,
            in_specs=[smem, smem, vmem, vmem, vmem],
            out_specs=[vmem] * len(outputs),
            scratch_shapes=scratch,
            compiler_params=pltpu.CompilerParams(
                collective_id=0, has_side_effects=True, vmem_limit_bytes=30 << 20),
            name="gram_exchange",
        )(doc_tokens, doc_shard, gate_pre, up_pre, grad_hidden)
        finish, scratch = make_finish(units, columns, TOK_DEV * shards)
        anywhere = pl.BlockSpec(memory_space=pl.ANY)
        act, grad = pl.pallas_call(
            finish,
            out_shape=[jax.ShapeDtypeStruct((units, 1, columns), jnp.float32)] * 2,
            in_specs=[vmem] * len(outputs),
            out_specs=[anywhere] * 2,
            scratch_shapes=scratch,
            compiler_params=pltpu.CompilerParams(vmem_limit_bytes=16 << 20),
            name="gram_finish",
        )(*panels)
        return act, grad

    return jax.shard_map(
        on_device,
        mesh=mesh,
        in_specs=(P("dp", "tile"), P("dp", "tile"), P("dp", "tile"), P(), P()),
        out_specs=(P("tile", "dp", None), P("tile", "dp", None)),
        check_vma=False,
    )
```

time: 154 us -> 111 us (0.72)
  Pallas kernels: 132 us -> 108 us
  local copies, waits for them, and re-layouts: 21.4 us -> 2.4 us
    pallas_call x1 -> x2, Pallas kernels: 132 us -> 108 us  [the longest x1 103 us: on_device(): pl.pallas_call(kernel, out_shape=outputs, in_specs=[smem, smem, vmem, vme...]
    unnamed x4 -> x6, local copies, waits for them, and re-layouts: 21.4 us -> 2.4 us
where the time goes in v2:
time: 111 us
  Pallas kernels  108 us (97%)
  local copies, waits for them, and re-layouts  2.4 us (2%)
    pallas_call x1, Pallas kernels, on_device(): pl.pallas_call(kernel, out_shape=outputs, in_specs=[smem, smem, vmem, vme...  103 us
    pallas_call x1, Pallas kernels, on_device(): pl.pallas_call(finish, out_shape=[jax.ShapeDtypeStruct((units, 1, columns...  4.77 us
    unnamed x6, local copies, waits for them, and re-layouts  2.4 us

profile of v2, /device:TPU:0, one launch (start us, length us, event | category | flops | bytes accessed | tf_op | source)
XLA Modules:
  0.0 111.2 jit_solution(849993303091686781)
XLA Ops:
  0.6 0.0 copy-start
  0.6 1.1 copy-done
  1.7 0.0 copy-start.1
  1.7 0.7 copy-done.1
  2.4 0.0 copy-start.2
  2.4 0.7 copy-done.2
  3.0 103.4 %gram_exchange.1 = (f32[896,1792]{1,0:T(8,128)S(1)}, f32[896,1792]{1,0:T(8,128)S(1)}, bf16[896,2048]{1,0:T(8,128)(2,1)S(1)}, bf16[1792,2048]{1,0:T(8,128)(2,1)S(1)}) custom-call(s32[32]{0:T(128)S(1)} %copy-done.1, s32[32]{0:T(128)S(1)} %copy-done.2, bf16[384,896]{1,0:T(8,128)(2,1)S(1)} %copy-done, bf16[384,896]{1,0:T(8,128)(2,1)} %up_ref.1, ...), custom_call_target="tpu_custom_call" | custom-call | tf_op jit(solution)/shard_map/gram_exchange/pallas_call | solution.py:399
  106.4 4.8 %gram_finish.1 = (f32[896,1,1792]{2,1,0:T(1,128)}, f32[896,1,1792]{2,1,0:T(1,128)}) custom-call(f32[896,1792]{1,0:T(8,128)S(1)} %get-tuple-element.6.act_in, f32[896,1792]{1,0:T(8,128)S(1)} %get-tuple-element.7.grad_in, bf16[896,2048]{1,0:T(8,128)(2,1)S(1)} %get-tuple-element.8.rp, bf16[1792,2048]{1,0:T(8,128)(2,1)S(1)} %get-tuple-element.9.cp), custom_call_target="tpu_custom_call" | custom-call | tf_op jit(solution)/shard_map/gram_finish/pallas_call | solution.py:411
Async XLA Ops:
  0.6 1.1 copy-start
  1.7 0.7 copy-start.1
  2.4 0.7 copy-start.2

commit v3 on v2

--- a/solution.py
+++ b/solution.py
@@ -32,7 +32,7 @@
         for shard in members:
             slots[n, shard] = len(slots)
     half = tokens // 2
-    cut = group * 3 // 7
+    cut = group * 2 // 7
     parts = [(0, 0, cut), (0, cut, group - cut), (1, 0, group)]
     pieces = []
     for f, top, rows in parts[:2]:
@@ -44,14 +44,18 @@
     pairs = [(i, i + 1) for i in range(0, len(pieces), 2)]
     columns = tiles * group
 
-    def kernel(tok_ref, own_ref, gate_ref, up_ref, down_ref, act_ref, grad_ref, rp1, cp1, xt, rv, perm, rp0, cp0,
+    def kernel(tok_ref, own_ref, gate_hbm, up_hbm, down_hbm, act_ref, grad_ref, rp1, cp1,
+               gate_ref, up_ref, down_ref, xt, rv, perm, rp0, cp0, load_s,
                swap_s, swap_r, local_s, row_s, row_r, col_s, col_r):
         outs, rp, cp = (act_ref, grad_ref), (rp0, rp1), (cp0, cp1)
-        sent = []
 
         def send(copy):
             copy.start()
-            sent.append(copy)
+
+        loads_in = [pltpu.make_async_copy(source, target, load_s.at[i]) for i, (source, target) in enumerate(
+            ((gate_hbm, gate_ref), (up_hbm, up_ref), (down_hbm, down_ref)))]
+        for copy in loads_in:
+            copy.start()
 
         dp, tile = lax.axis_index("dp"), lax.axis_index("tile")
         y, core = dp // 2, lax.rem(dp, 2)
@@ -114,12 +118,19 @@
         def rows_of(index, top, rows):
             return pl.ds(pl.multiple_of(index * group + top, 16), rows)
 
-        def swap(part, o, source, home):
+        def swap(part, o):
             f, top, rows = parts[part]
             return pltpu.make_async_remote_copy(
-                src_ref=xt.at[f, rows_of(home, top, rows)], dst_ref=rv.at[f, source, pl.ds(top, rows)],
-                send_sem=swap_s.at[part, o], recv_sem=swap_r.at[part, o],
+                src_ref=xt.at[f, rows_of(over_dp(o), top, rows)], dst_ref=rv.at[f, dp, pl.ds(top, rows)],
+                send_sem=swap_s.at[part], recv_sem=swap_r.at[part],
                 device_id=(over_dp(o), tile), device_id_type=MESH)
+
+        def swap_all(part):
+            f, top, rows = parts[part]
+            both = rv.at[f, pl.ds(0, shards - 1), pl.ds(top, rows)]
+            return pltpu.make_async_remote_copy(
+                src_ref=both, dst_ref=both, send_sem=swap_s.at[part], recv_sem=swap_r.at[part],
+                device_id=(over_dp(1), tile), device_id_type=MESH)
 
         def swap_own(part):
             f, top, rows = parts[part]
@@ -128,13 +139,12 @@
 
         def start_swap(part):
             for o in (3, 4, 5, 2, 6, 7, 1):
-                send(swap(part, o, dp, over_dp(o)))
+                swap(part, o).start()
             swap_own(part).start()
 
         def end_swap(part):
             swap_own(part).wait()
-            for o in range(1, shards):
-                swap(part, o, over_dp(-o), dp).wait_recv()
+            swap_all(part).wait_recv()
 
         def build_perm():
             diff = (lax.broadcasted_iota(jnp.int32, (capacity, WIDE), 1)
@@ -159,7 +169,7 @@
             lanes = pl.ds((index - 2) * half, half) if index in (2, 3) else slice(None)
             part = rp[f].at[at_group(origin), lanes]
             return pltpu.make_async_remote_copy(
-                src_ref=part, dst_ref=part, send_sem=row_s.at[f, index], recv_sem=row_r.at[f, index],
+                src_ref=part, dst_ref=part, send_sem=row_s.at[f], recv_sem=row_r.at[f, index],
                 device_id=peer, device_id_type=MESH)
 
         def same_core(d):
@@ -181,9 +191,21 @@
                 row(f, index, same_core(2), sibling).wait_recv()
             send(row(f, 7, same_core(2), sibling))
 
+        def row_sent(f):
+            whole = rp[f].at[pl.ds(0, 7 * group)]
+            pltpu.make_async_remote_copy(
+                src_ref=whole, dst_ref=whole, send_sem=row_s.at[f], recv_sem=row_r.at[f, 0],
+                device_id=sibling, device_id_type=MESH).wait_send()
+
         def row_end(f):
             for index, d in ((4, 0), (5, -1), (6, 1), (7, 2)):
                 row(f, index, plus(y, d) * 2 + 1 - core, sibling).wait_recv()
+
+        def arrival(index):
+            kind, b = index % 4, index // 4
+            if kind < 2:
+                return 2 * b + kind
+            return 10 if b == 0 else 11
 
         def column(piece, index, origin, peer):
             f, top, rows, start, wide = pieces[piece]
@@ -193,17 +215,30 @@
                 start += (kind - 2) * wide
             part = cp[f].at[rows_of(origin, top, rows), pl.ds(start, wide)]
             return pltpu.make_async_remote_copy(
-                src_ref=part, dst_ref=part, send_sem=col_s.at[piece, index], recv_sem=col_r.at[piece, index],
+                src_ref=part, dst_ref=part, send_sem=col_s.at[piece], recv_sem=col_r.at[piece, arrival(index)],
                 device_id=(dp, peer), device_id_type=MESH)
+
+        def column_all(piece, index, count):
+            f, top, rows, start, wide = pieces[piece]
+            part = cp[f].at[pl.ds(0, count * rows), pl.ds(start, wide)]
+            return pltpu.make_async_remote_copy(
+                src_ref=part, dst_ref=part, send_sem=col_s.at[piece], recv_sem=col_r.at[piece, arrival(index)],
+                device_id=(dp, tile), device_id_type=MESH)
 
         def place(piece, d1, d2):
             return plane(piece % 2 == 0, d1, d2)
 
-        def col_out(p):
+        def col_first(p):
             for index, d in ((0, 1), (1, -1)):
                 send(column(p, index, tile, place(p, d, 0)))
+
+        def col_second(p):
             for index, d in ((4, 1), (5, -1)):
                 send(column(p, index, tile, place(p, 0, d)))
+
+        def col_out(pair):
+            each(col_first, pair)
+            each(col_second, pair)
 
         def col_near(p):
             for index, d in ((0, 1), (1, -1)):
@@ -217,8 +252,7 @@
 
         def col_far(p):
             origin = place(p, 2, 0)
-            for index in (2, 3):
-                column(p, index, origin, tile).wait_recv()
+            column_all(p, 2, 1).wait_recv()
             send(column(p, 12, origin, place(p, 0, 1)))
             send(column(p, 13, origin, place(p, 0, -1)))
 
@@ -229,9 +263,7 @@
                 send(column(p, 6 + 4 * b + index, origin, place(p, 0, d)))
 
         def col_end(p):
-            for b in range(SIDE):
-                for index in (2, 3):
-                    column(p, 4 + 4 * b + index, place(p, -b, 2), tile).wait_recv()
+            column_all(p, 6, SIDE).wait_recv()
 
         def multiply(f, start, wide, first, last):
             ks = pl.ds(start, wide)
@@ -253,79 +285,88 @@
             for p in pairs[pair]:
                 act(p, *more)
 
+        loads_in[0].wait()
+        loads_in[1].wait()
         lax.fori_loop(0, units // 128, make_hidden, 0)
         pl.semaphore_wait(barrier, len(peers))
         start_swap(0)
         build_perm()
+        loads_in[2].wait()
+        lax.fori_loop(0, units // 128, make_dgate, 0)
         end_swap(0)
         start_swap(1)
         for p in pairs[0]:
             pack(p)
-            col_out(p)
-        lax.fori_loop(0, units // 128, make_dgate, 0)
+            col_first(p)
+        each(col_second, 0)
+        each(col_near, 0)
         end_swap(1)
         start_swap(2)
-        each(pack, 1)
-        each(col_near, 0)
-        each(col_out, 1)
+        for p in pairs[1]:
+            pack(p)
+            col_first(p)
+        each(col_second, 1)
         each(col_pass, 0, 0)
         each(col_far, 0)
+        each(col_pass, 0, 1)
+        each(col_pass, 0, 3)
+        each(col_near, 1)
+        each(col_pass, 0, 2)
         end_swap(2)
         row_out(0)
-        each(col_pass, 0, 1)
-        each(col_pass, 0, 3)
         each(pack, 2)
+        col_out(2)
+        each(col_pass, 1, 0)
+        each(col_far, 1)
         each(pack, 3)
         each(pack, 4)
-        each(col_pass, 0, 2)
-        each(col_near, 1)
-        each(col_out, 2)
         row_pass(0)
-        each(col_pass, 1, 0)
-        each(col_far, 1)
         each(col_pass, 1, 1)
+        each(col_pass, 1, 3)
+        each(col_near, 2)
         row_far(0)
         row_out(1)
-        each(col_pass, 1, 3)
         each(col_pass, 1, 2)
+        col_out(3)
         row_end(0)
-        each(col_near, 2)
-        each(col_out, 3)
+        each(col_pass, 2, 0)
+        each(col_far, 2)
         each(col_end, 0)
         each(col_end, 1)
-        multiply(0, 0, tokens, 0, 2)
+        multiply(0, 0, tokens, 0, 3)
         row_pass(1)
-        each(col_pass, 2, 0)
-        each(col_far, 2)
-        multiply(0, 0, tokens, 2, 4)
         each(col_pass, 2, 1)
+        each(col_near, 3)
         each(col_pass, 2, 3)
-        multiply(0, 0, tokens, 4, 5)
+        col_out(4)
+        multiply(0, 0, tokens, 3, 5)
         row_far(1)
         each(col_pass, 2, 2)
-        each(col_near, 3)
-        each(col_out, 4)
+        each(col_pass, 3, 0)
+        each(col_far, 3)
+        each(col_near, 4)
         multiply(0, 0, tokens, 5, 7)
         row_end(1)
-        each(col_pass, 3, 0)
-        each(col_far, 3)
-        each(col_end, 2)
         each(col_pass, 3, 1)
         each(col_pass, 3, 3)
-        multiply(1, 0, 2 * F1_WIDTHS[0], 0, 4)
-        each(col_pass, 3, 2)
-        each(col_near, 4)
-        multiply(1, 0, 2 * F1_WIDTHS[0], 4, 7)
         each(col_pass, 4, 0)
         each(col_far, 4)
+        each(col_end, 2)
+        multiply(1, 0, 2 * F1_WIDTHS[0], 0, 3)
+        each(col_pass, 3, 2)
         each(col_pass, 4, 1)
         each(col_pass, 4, 3)
+        multiply(1, 0, 2 * F1_WIDTHS[0], 3, 7)
         each(col_pass, 4, 2)
         each(col_end, 3)
         multiply(1, 2 * F1_WIDTHS[0], 2 * F1_WIDTHS[1], 0, 7)
         each(col_end, 4)
-        for copy in sent:
-            copy.wait_send()
+        for part in range(len(parts)):
+            swap_all(part).wait_send()
+        for f in range(2):
+            row_sent(f)
+        for p in range(len(pieces)):
+            column_all(p, 0, 15).wait_send()
 
     vmem = pltpu.VMEM
     outputs = [
@@ -334,19 +375,20 @@
         vmem((units, tokens), jnp.bfloat16),
         vmem((columns, tokens), jnp.bfloat16),
     ]
-    scratch = [
+    scratch = [vmem((capacity, units), jnp.bfloat16)] * 3 + [
         vmem((2, units, capacity), jnp.bfloat16),
         vmem((2, shards, group, capacity), jnp.bfloat16),
         vmem((len(slots), capacity, WIDE), jnp.bfloat16),
         vmem((units, tokens), jnp.bfloat16),
         vmem((columns, tokens), jnp.bfloat16),
-        pltpu.SemaphoreType.DMA((len(parts), shards)),
-        pltpu.SemaphoreType.DMA((len(parts), shards)),
+        pltpu.SemaphoreType.DMA((3,)),
         pltpu.SemaphoreType.DMA((len(parts),)),
+        pltpu.SemaphoreType.DMA((len(parts),)),
+        pltpu.SemaphoreType.DMA((len(parts),)),
+        pltpu.SemaphoreType.DMA((2,)),
         pltpu.SemaphoreType.DMA((2, 8)),
-        pltpu.SemaphoreType.DMA((2, 8)),
-        pltpu.SemaphoreType.DMA((len(pieces), 20)),
-        pltpu.SemaphoreType.DMA((len(pieces), 20)),
+        pltpu.SemaphoreType.DMA((len(pieces),)),
+        pltpu.SemaphoreType.DMA((len(pieces), 12)),
     ]
     return kernel, outputs, scratch
 
@@ -396,16 +438,18 @@
         columns = tiles * group
         kernel, outputs, scratch = make_kernel(capacity, units, group, shards, tiles)
         smem, vmem = pl.BlockSpec(memory_space=pltpu.SMEM), pl.BlockSpec(memory_space=pltpu.VMEM)
+        hbm = pl.BlockSpec(memory_space=pltpu.HBM)
         panels = pl.pallas_call(
             kernel,
             out_shape=outputs,
-            in_specs=[smem, smem, vmem, vmem, vmem],
+            in_specs=[smem, smem, hbm, hbm, hbm],
             out_specs=[vmem] * len(outputs),
             scratch_shapes=scratch,
             compiler_params=pltpu.CompilerParams(
                 collective_id=0, has_side_effects=True, vmem_limit_bytes=30 << 20),
             name="gram_exchange",
-        )(doc_tokens, doc_shard, gate_pre, up_pre, grad_hidden)
+        )(*(pltpu.with_memory_space_constraint(v, pltpu.HBM)
+            for v in (doc_tokens, doc_shard, gate_pre, up_pre, grad_hidden)))
         finish, scratch = make_finish(units, columns, TOK_DEV * shards)
         anywhere = pl.BlockSpec(memory_space=pl.ANY)
         act, grad = pl.pallas_call(

time: 111 us -> 101 us (0.910)
  Pallas kernels: 108 us -> 100 us
  local copies, waits for them, and re-layouts: 2.4 us -> 0 us
    pallas_call x1, Pallas kernels: 103 us -> 95.2 us  [on_device(): pl.pallas_call(kernel, out_shape=outputs, in_specs=[smem, smem, hbm, hbm,...]
    unnamed x6 -> x0, local copies, waits for them, and re-layouts: 2.4 us -> none
where the time goes in v3:
time: 101 us
  Pallas kernels  100 us (99%)
    pallas_call x1, Pallas kernels, on_device(): pl.pallas_call(kernel, out_shape=outputs, in_specs=[smem, smem, hbm, hbm,...  95.2 us
    pallas_call x1, Pallas kernels, on_device(): pl.pallas_call(finish, out_shape=[jax.ShapeDtypeStruct((units, 1, columns...  4.77 us

profile of v3, /device:TPU:0, one launch (start us, length us, event | category | flops | bytes accessed | tf_op | source)
XLA Modules:
  0.0 100.6 jit_solution(12969938019911182939)
XLA Ops:
  0.6 95.2 %gram_exchange.1 = (f32[896,1792]{1,0:T(8,128)S(1)}, f32[896,1792]{1,0:T(8,128)S(1)}, bf16[896,2048]{1,0:T(8,128)(2,1)S(1)}, bf16[1792,2048]{1,0:T(8,128)(2,1)S(1)}) custom-call(s32[32]{0:T(128)} %tok_ref.1, s32[32]{0:T(128)} %own_ref.1, bf16[384,896]{1,0:T(8,128)(2,1)} %gate_hbm.1, bf16[384,896]{1,0:T(8,128)(2,1)} %up_hbm.1, bf16[384,896]{1,0:T(8,128)(2,1)} %down_hbm.1), custom_call_target="tpu_custom_call" | custom-call | tf_op jit(solution)/shard_map/gram_exchange/pallas_call | solution.py:442
  95.8 4.8 %gram_finish.1 = (f32[896,1,1792]{2,1,0:T(1,128)}, f32[896,1,1792]{2,1,0:T(1,128)}) custom-call(f32[896,1792]{1,0:T(8,128)S(1)} %get-tuple-element.6.act_in, f32[896,1792]{1,0:T(8,128)S(1)} %get-tuple-element.7.grad_in, bf16[896,2048]{1,0:T(8,128)(2,1)S(1)} %get-tuple-element.8.rp, bf16[1792,2048]{1,0:T(8,128)(2,1)S(1)} %get-tuple-element.9.cp), custom_call_target="tpu_custom_call" | custom-call | tf_op jit(solution)/shard_map/gram_finish/pallas_call | solution.py:455

commit v4 on v3

--- a/solution.py
+++ b/solution.py
@@ -52,10 +52,23 @@
         def send(copy):
             copy.start()
 
-        loads_in = [pltpu.make_async_copy(source, target, load_s.at[i]) for i, (source, target) in enumerate(
-            ((gate_hbm, gate_ref), (up_hbm, up_ref), (down_hbm, down_ref)))]
-        for copy in loads_in:
-            copy.start()
+        def fetch(i, b):
+            cols = pl.ds(pl.multiple_of(b * 128, 128), 128)
+            source = (gate_hbm, up_hbm, down_hbm)[i]
+            target = (gate_ref, up_ref, down_ref)[i]
+            return pltpu.make_async_copy(source.at[:, cols], target.at[:, cols], load_s.at[i, b])
+
+        def fetch_pair(b, _):
+            fetch(0, b).start()
+            fetch(1, b).start()
+            return 0
+
+        def fetch_down(b, _):
+            fetch(2, b).start()
+            return 0
+
+        lax.fori_loop(0, units // 128, fetch_pair, 0)
+        lax.fori_loop(0, units // 128, fetch_down, 0)
 
         dp, tile = lax.axis_index("dp"), lax.axis_index("tile")
         y, core = dp // 2, lax.rem(dp, 2)
@@ -95,6 +108,8 @@
         live = lax.broadcasted_iota(jnp.int32, (capacity, 128), 0) < own_load
 
         def make_hidden(b, _):
+            fetch(0, b).wait()
+            fetch(1, b).wait()
             cols = pl.ds(pl.multiple_of(b * 128, 128), 128)
             g = gate_ref[:, cols].astype(jnp.float32)
             u = up_ref[:, cols].astype(jnp.float32)
@@ -103,6 +118,7 @@
             return 0
 
         def make_dgate(b, _):
+            fetch(2, b).wait()
             cols = pl.ds(pl.multiple_of(b * 128, 128), 128)
             g = gate_ref[:, cols].astype(jnp.float32)
             u = up_ref[:, cols].astype(jnp.float32)
@@ -268,15 +284,15 @@
         def multiply(f, start, wide, first, last):
             ks = pl.ds(start, wide)
 
-            def step(n, _):
-                cols = pl.ds(pl.multiple_of(n * WIDE, WIDE), WIDE)
-                gram = lax.dot_general(rp[f][:, ks], cp[f][cols, ks], (((1,), (1,)), ((), ())),
+            def step(i, _):
+                part = pl.ds(pl.multiple_of(i * (units // 2), 16), units // 2)
+                gram = lax.dot_general(rp[f][part, ks], cp[f][:, ks], (((1,), (1,)), ((), ())),
                                        preferred_element_type=jnp.float32)
                 if start > 0:
-                    gram = outs[f][:, cols] + gram
+                    gram = outs[f][part] + gram
                 if start + wide == tokens:
                     gram = gram * (1.0 / tokens)
-                outs[f][:, cols] = gram
+                outs[f][part] = gram
                 return 0
 
             lax.fori_loop(first, last, step, 0)
@@ -285,13 +301,10 @@
             for p in pairs[pair]:
                 act(p, *more)
 
-        loads_in[0].wait()
-        loads_in[1].wait()
         lax.fori_loop(0, units // 128, make_hidden, 0)
         pl.semaphore_wait(barrier, len(peers))
         start_swap(0)
         build_perm()
-        loads_in[2].wait()
         lax.fori_loop(0, units // 128, make_dgate, 0)
         end_swap(0)
         start_swap(1)
@@ -300,66 +313,67 @@
             col_first(p)
         each(col_second, 0)
         each(col_near, 0)
+        each(col_pass, 0, 0)
         end_swap(1)
         start_swap(2)
         for p in pairs[1]:
             pack(p)
             col_first(p)
+        each(col_far, 0)
         each(col_second, 1)
-        each(col_pass, 0, 0)
-        each(col_far, 0)
         each(col_pass, 0, 1)
+        each(col_near, 1)
         each(col_pass, 0, 3)
-        each(col_near, 1)
         each(col_pass, 0, 2)
         end_swap(2)
         row_out(0)
-        each(pack, 2)
-        col_out(2)
+        for p in pairs[2]:
+            pack(p)
+            col_first(p)
+        each(col_second, 2)
         each(col_pass, 1, 0)
         each(col_far, 1)
         each(pack, 3)
         each(pack, 4)
+        each(col_near, 2)
+        each(col_pass, 1, 1)
         row_pass(0)
-        each(col_pass, 1, 1)
+        each(col_first, 3)
         each(col_pass, 1, 3)
-        each(col_near, 2)
+        each(col_second, 3)
+        each(col_pass, 1, 2)
         row_far(0)
         row_out(1)
-        each(col_pass, 1, 2)
-        col_out(3)
+        each(col_near, 3)
         row_end(0)
         each(col_pass, 2, 0)
         each(col_far, 2)
+        each(col_first, 4)
         each(col_end, 0)
         each(col_end, 1)
-        multiply(0, 0, tokens, 0, 3)
+        multiply(0, 0, tokens, 0, 1)
+        each(col_pass, 2, 1)
+        each(col_second, 4)
         row_pass(1)
-        each(col_pass, 2, 1)
-        each(col_near, 3)
         each(col_pass, 2, 3)
-        col_out(4)
-        multiply(0, 0, tokens, 3, 5)
+        each(col_near, 4)
+        multiply(0, 0, tokens, 1, 2)
+        each(col_far, 3)
+        each(col_pass, 2, 2)
         row_far(1)
-        each(col_pass, 2, 2)
         each(col_pass, 3, 0)
-        each(col_far, 3)
-        each(col_near, 4)
-        multiply(0, 0, tokens, 5, 7)
+        each(col_pass, 3, 1)
+        each(col_far, 4)
+        each(col_end, 2)
         row_end(1)
-        each(col_pass, 3, 1)
         each(col_pass, 3, 3)
         each(col_pass, 4, 0)
-        each(col_far, 4)
-        each(col_end, 2)
-        multiply(1, 0, 2 * F1_WIDTHS[0], 0, 3)
         each(col_pass, 3, 2)
         each(col_pass, 4, 1)
         each(col_pass, 4, 3)
-        multiply(1, 0, 2 * F1_WIDTHS[0], 3, 7)
         each(col_pass, 4, 2)
+        multiply(1, 0, 2 * F1_WIDTHS[0], 0, 2)
         each(col_end, 3)
-        multiply(1, 2 * F1_WIDTHS[0], 2 * F1_WIDTHS[1], 0, 7)
         each(col_end, 4)
         for part in range(len(parts)):
             swap_all(part).wait_send()
@@ -381,7 +395,7 @@
         vmem((len(slots), capacity, WIDE), jnp.bfloat16),
         vmem((units, tokens), jnp.bfloat16),
         vmem((columns, tokens), jnp.bfloat16),
-        pltpu.SemaphoreType.DMA((3,)),
+        pltpu.SemaphoreType.DMA((3, units // 128)),
         pltpu.SemaphoreType.DMA((len(parts),)),
         pltpu.SemaphoreType.DMA((len(parts),)),
         pltpu.SemaphoreType.DMA((len(parts),)),
@@ -394,37 +408,35 @@
 
 
 def make_finish(units, columns, tokens):
-    last = 2 * F1_WIDTHS[-1]
+    last = 2 * sum(F1_WIDTHS[1:])
 
     def finish(act_in, grad_in, rp, cp, act_ref, grad_ref, total, act_s, grad_s):
         act_out = pltpu.make_async_copy(act_in, act_ref.at[:, 0, :], act_s)
         act_out.start()
 
-        def copy(n):
-            cols = pl.ds(pl.multiple_of(n * WIDE, WIDE), WIDE)
-            return pltpu.make_async_copy(total.at[:, cols], grad_ref.at[:, 0, cols], grad_s.at[n])
-
-        def step(n, _):
-            cols = pl.ds(pl.multiple_of(n * WIDE, WIDE), WIDE)
+        def half(i):
+            return pl.ds(pl.multiple_of(i * (units // 2), 16), units // 2)
+
+        def copy(i):
+            return pltpu.make_async_copy(total.at[half(i)], grad_ref.at[half(i), 0, :], grad_s.at[i])
+
+        def step(i, _):
             ks = pl.ds(tokens - last, last)
-            gram = lax.dot_general(rp[:, ks], cp[cols, ks], (((1,), (1,)), ((), ())),
+            gram = lax.dot_general(rp[half(i), ks], cp[:, ks], (((1,), (1,)), ((), ())),
                                    preferred_element_type=jnp.float32)
-            total[:, cols] = (grad_in[:, cols] + gram) * (1.0 / tokens)
-            copy(n).start()
+            total[half(i)] = (grad_in[half(i)] + gram) * (1.0 / tokens)
+            copy(i).start()
             return 0
 
-        def wait(n, _):
-            copy(n).wait()
-            return 0
-
-        lax.fori_loop(0, columns // WIDE, step, 0)
-        lax.fori_loop(0, columns // WIDE, wait, 0)
+        lax.fori_loop(0, 2, step, 0)
+        for i in range(2):
+            copy(i).wait()
         act_out.wait()
 
     scratch = [
         pltpu.VMEM((units, columns), jnp.float32),
         pltpu.SemaphoreType.DMA,
-        pltpu.SemaphoreType.DMA((columns // WIDE,)),
+        pltpu.SemaphoreType.DMA((2,)),
     ]
     return finish, scratch
 

time: 101 us -> 98.9 us (0.979)
  Pallas kernels: 100 us -> 98 us
    pallas_call x1, Pallas kernels: 95.2 us -> 92.5 us  [on_device(): pl.pallas_call(kernel, out_shape=outputs, in_specs=[smem, smem, hbm, hbm,...]
where the time goes in v4:
time: 98.9 us; the launch traced here: 98.8 us
  Pallas kernels  98 us (99%)
    pallas_call x1, Pallas kernels, on_device(): pl.pallas_call(kernel, out_shape=outputs, in_specs=[smem, smem, hbm, hbm,...  92.5 us
    pallas_call x1, Pallas kernels, on_device(): pl.pallas_call(finish, out_shape=[jax.ShapeDtypeStruct((units, 1, columns...  5.46 us

profile of v4, /device:TPU:0, one launch (start us, length us, event | category | flops | bytes accessed | tf_op | source)
XLA Modules:
  0.0 98.8 jit_solution(14341702686223688069)
XLA Ops:
  0.6 92.5 %gram_exchange.1 = (f32[896,1792]{1,0:T(8,128)S(1)}, f32[896,1792]{1,0:T(8,128)S(1)}, bf16[896,2048]{1,0:T(8,128)(2,1)S(1)}, bf16[1792,2048]{1,0:T(8,128)(2,1)S(1)}) custom-call(s32[32]{0:T(128)} %tok_ref.1, s32[32]{0:T(128)} %own_ref.1, bf16[384,896]{1,0:T(8,128)(2,1)} %gate_hbm.1, bf16[384,896]{1,0:T(8,128)(2,1)} %up_hbm.1, bf16[384,896]{1,0:T(8,128)(2,1)} %down_hbm.1), custom_call_target="tpu_custom_call" | custom-call | tf_op jit(solution)/shard_map/gram_exchange/pallas_call | solution.py:454
  93.2 5.5 %gram_finish.1 = (f32[896,1,1792]{2,1,0:T(1,128)}, f32[896,1,1792]{2,1,0:T(1,128)}) custom-call(f32[896,1792]{1,0:T(8,128)S(1)} %get-tuple-element.6.act_in, f32[896,1792]{1,0:T(8,128)S(1)} %get-tuple-element.7.grad_in, bf16[896,2048]{1,0:T(8,128)(2,1)S(1)} %get-tuple-element.8.rp, bf16[1792,2048]{1,0:T(8,128)(2,1)S(1)} %get-tuple-element.9.cp), custom_call_target="tpu_custom_call" | custom-call | tf_op jit(solution)/shard_map/gram_finish/pallas_call | solution.py:467

commit v5 on v4

--- a/solution.py
+++ b/solution.py
@@ -8,7 +8,7 @@
 MESH = pl.DeviceIdType.MESH
 TOK_DEV = 256
 DOCS_SHARD = 4
-F1_WIDTHS = (512, 256, 256)
+F1_WIDTHS = (512, 512)
 WIDE = 256
 SIDE = 4
 
@@ -334,7 +334,6 @@
         each(col_pass, 1, 0)
         each(col_far, 1)
         each(pack, 3)
-        each(pack, 4)
         each(col_near, 2)
         each(col_pass, 1, 1)
         row_pass(0)
@@ -348,33 +347,24 @@
         row_end(0)
         each(col_pass, 2, 0)
         each(col_far, 2)
-        each(col_first, 4)
         each(col_end, 0)
         each(col_end, 1)
         multiply(0, 0, tokens, 0, 1)
         each(col_pass, 2, 1)
-        each(col_second, 4)
         row_pass(1)
+        each(col_far, 3)
         each(col_pass, 2, 3)
-        each(col_near, 4)
         multiply(0, 0, tokens, 1, 2)
-        each(col_far, 3)
         each(col_pass, 2, 2)
         row_far(1)
         each(col_pass, 3, 0)
         each(col_pass, 3, 1)
-        each(col_far, 4)
+        each(col_pass, 3, 3)
+        row_end(1)
+        each(col_pass, 3, 2)
         each(col_end, 2)
-        row_end(1)
-        each(col_pass, 3, 3)
-        each(col_pass, 4, 0)
-        each(col_pass, 3, 2)
-        each(col_pass, 4, 1)
-        each(col_pass, 4, 3)
-        each(col_pass, 4, 2)
         multiply(1, 0, 2 * F1_WIDTHS[0], 0, 2)
         each(col_end, 3)
-        each(col_end, 4)
         for part in range(len(parts)):
             swap_all(part).wait_send()
         for f in range(2):

time: 98.9 us -> 97.4 us (0.985)
  Pallas kernels: 98 us -> 96.5 us
    pallas_call x1, Pallas kernels: 92.5 us -> 91 us  [on_device(): pl.pallas_call(kernel, out_shape=outputs, in_specs=[smem, smem, hbm, hbm,...]
where the time goes in v5:
time: 97.4 us; the launch traced here: 97.3 us
  Pallas kernels  96.5 us (99%)
    pallas_call x1, Pallas kernels, on_device(): pl.pallas_call(kernel, out_shape=outputs, in_specs=[smem, smem, hbm, hbm,...  91 us
    pallas_call x1, Pallas kernels, on_device(): pl.pallas_call(finish, out_shape=[jax.ShapeDtypeStruct((units, 1, columns...  5.46 us

profile of v5, /device:TPU:0, one launch (start us, length us, event | category | flops | bytes accessed | tf_op | source)
XLA Modules:
  0.0 97.3 jit_solution(14589497188410732053)
XLA Ops:
  0.6 91.0 %gram_exchange.1 = (f32[896,1792]{1,0:T(8,128)S(1)}, f32[896,1792]{1,0:T(8,128)S(1)}, bf16[896,2048]{1,0:T(8,128)(2,1)S(1)}, bf16[1792,2048]{1,0:T(8,128)(2,1)S(1)}) custom-call(s32[32]{0:T(128)} %tok_ref.1, s32[32]{0:T(128)} %own_ref.1, bf16[384,896]{1,0:T(8,128)(2,1)} %gate_hbm.1, bf16[384,896]{1,0:T(8,128)(2,1)} %up_hbm.1, bf16[384,896]{1,0:T(8,128)(2,1)} %down_hbm.1), custom_call_target="tpu_custom_call" | custom-call | tf_op jit(solution)/shard_map/gram_exchange/pallas_call | solution.py:444
  91.6 5.5 %gram_finish.1 = (f32[896,1,1792]{2,1,0:T(1,128)}, f32[896,1,1792]{2,1,0:T(1,128)}) custom-call(f32[896,1792]{1,0:T(8,128)S(1)} %get-tuple-element.6.act_in, f32[896,1792]{1,0:T(8,128)S(1)} %get-tuple-element.7.grad_in, bf16[896,2048]{1,0:T(8,128)(2,1)S(1)} %get-tuple-element.8.rp, bf16[1792,2048]{1,0:T(8,128)(2,1)S(1)} %get-tuple-element.9.cp), custom_call_target="tpu_custom_call" | custom-call | tf_op jit(solution)/shard_map/gram_finish/pallas_call | solution.py:457

commit v6 on v5

--- a/solution.py
+++ b/solution.py
@@ -404,29 +404,24 @@
         act_out = pltpu.make_async_copy(act_in, act_ref.at[:, 0, :], act_s)
         act_out.start()
 
-        def half(i):
-            return pl.ds(pl.multiple_of(i * (units // 2), 16), units // 2)
-
-        def copy(i):
-            return pltpu.make_async_copy(total.at[half(i)], grad_ref.at[half(i), 0, :], grad_s.at[i])
-
-        def step(i, _):
-            ks = pl.ds(tokens - last, last)
-            gram = lax.dot_general(rp[half(i), ks], cp[:, ks], (((1,), (1,)), ((), ())),
+        ks = pl.ds(tokens - last, last)
+        copies = []
+        for first, wide in ((0, 3 * WIDE), (3 * WIDE, 2 * WIDE), (5 * WIDE, 2 * WIDE)):
+            cols = pl.ds(first, wide)
+            gram = lax.dot_general(rp[:, ks], cp[cols, ks], (((1,), (1,)), ((), ())),
                                    preferred_element_type=jnp.float32)
-            total[half(i)] = (grad_in[half(i)] + gram) * (1.0 / tokens)
-            copy(i).start()
-            return 0
-
-        lax.fori_loop(0, 2, step, 0)
-        for i in range(2):
-            copy(i).wait()
+            total[:, cols] = (grad_in[:, cols] + gram) * (1.0 / tokens)
+            copies.append(pltpu.make_async_copy(
+                total.at[:, cols], grad_ref.at[:, 0, cols], grad_s.at[len(copies)]))
+            copies[-1].start()
+        for copy in copies:
+            copy.wait()
         act_out.wait()
 
     scratch = [
         pltpu.VMEM((units, columns), jnp.float32),
         pltpu.SemaphoreType.DMA,
-        pltpu.SemaphoreType.DMA((2,)),
+        pltpu.SemaphoreType.DMA((3,)),
     ]
     return finish, scratch
 

time: 97.4 us -> 97.2 us (level)
  no operation moved by 1% of the time
where the time goes in v6:
time: 97.2 us; the launch traced here: 97 us
  Pallas kernels  96.2 us (99%)
    pallas_call x1, Pallas kernels, on_device(): pl.pallas_call(kernel, out_shape=outputs, in_specs=[smem, smem, hbm, hbm,...  91 us
    pallas_call x1, Pallas kernels, on_device(): pl.pallas_call(finish, out_shape=[jax.ShapeDtypeStruct((units, 1, columns...  5.18 us

profile of v6, /device:TPU:0, one launch (start us, length us, event | category | flops | bytes accessed | tf_op | source)
XLA Modules:
  0.0 97.0 jit_solution(3848094146928355825)
XLA Ops:
  0.6 91.0 %gram_exchange.1 = (f32[896,1792]{1,0:T(8,128)S(1)}, f32[896,1792]{1,0:T(8,128)S(1)}, bf16[896,2048]{1,0:T(8,128)(2,1)S(1)}, bf16[1792,2048]{1,0:T(8,128)(2,1)S(1)}) custom-call(s32[32]{0:T(128)} %tok_ref.1, s32[32]{0:T(128)} %own_ref.1, bf16[384,896]{1,0:T(8,128)(2,1)} %gate_hbm.1, bf16[384,896]{1,0:T(8,128)(2,1)} %up_hbm.1, bf16[384,896]{1,0:T(8,128)(2,1)} %down_hbm.1), custom_call_target="tpu_custom_call" | custom-call | tf_op jit(solution)/shard_map/gram_exchange/pallas_call | solution.py:439
  91.6 5.2 %gram_finish.1 = (f32[896,1,1792]{2,1,0:T(1,128)}, f32[896,1,1792]{2,1,0:T(1,128)}) custom-call(f32[896,1792]{1,0:T(8,128)S(1)} %get-tuple-element.6.act_in, f32[896,1792]{1,0:T(8,128)S(1)} %get-tuple-element.7.grad_in, bf16[896,2048]{1,0:T(8,128)(2,1)S(1)} %get-tuple-element.8.rp, bf16[1792,2048]{1,0:T(8,128)(2,1)S(1)} %get-tuple-element.9.cp), custom_call_target="tpu_custom_call" | custom-call | tf_op jit(solution)/shard_map/gram_finish/pallas_call | solution.py:452
